TPU v7x, 512 devices: a whole 4x4x16 slice. The times are simulated.
512 devices in a mesh: dp: 32 (over z_hi, x, y), seq: 16 (over z_lo, core).
Axes of the slice: x: 4, y: 4, z: 16 (z_hi: 2, z_lo: 8; z = z_hi * 8 + z_lo), core: 2. Of those that a mesh axis runs over, the one named last changes fastest.
Arguments:
- tokens: bfloat16 [32, 4096, 1280], P('dp', 'seq'), may hold values from -6 to 6
- out_grad: bfloat16 [32, 4096, 1280], P('dp', 'seq'), may hold values from -6 to 6
- logits: float32 [32, 16, 4096], P('dp', None, 'seq'), may hold values from -40 to 300
- router: bfloat16 [16, 1280], replicated, may hold values from -0.15625 to 0.15625
- w_in: bfloat16 [16, 1280, 5120], P('seq', None, 'dp'), may hold values from -0.15625 to 0.15625
- w_out: bfloat16 [16, 5120, 1280], P('seq', 'dp'), may hold values from -0.078125 to 0.078125
Outputs:
- token_grad: bfloat16 [32, 4096, 1280], P('dp', 'seq')
- router_grad: float32 [16, 1280], replicated
- w_in_grad: bfloat16 [16, 1280, 5120], P('seq', None, 'dp')
- w_out_grad: bfloat16 [16, 5120, 1280], P('seq', 'dp')
All inputs are finite; a program needn't handle non-finite values.
Results may differ from a plain program's by a relative error of at most 0.022.
Values may be sent and summed in bfloat16 or wider, within the bound.
A program may use at most 64 MiB of HBM per device.

v0:
```python
import math

import jax
import jax.numpy as jnp
from jax import lax
from jax.sharding import PartitionSpec as P


def contract_first(left, right):
    return lax.dot_general(
        left, right, (((0,), (0,)), ((), ())), preferred_element_type=jnp.float32
    )


def contract_last(left, right):
    return lax.dot_general(
        left, right, (((1,), (1,)), ((), ())), preferred_element_type=jnp.float32
    )


def local(tokens, out_grad, logits, router, w_in, w_out):
    tokens_local = tokens[0]
    grads_local = out_grad[0]
    logit_rows = logits[0]
    width = tokens_local.shape[1]
    owned = w_in.shape[0]
    combine = jax.nn.softmax(logit_rows, axis=0)
    combine_low = combine.astype(jnp.bfloat16)
    col_peak = lax.pmax(jnp.max(logit_rows, axis=1), "seq")
    raised = jnp.exp(logit_rows - col_peak[:, None])
    col_total = lax.psum(jnp.sum(raised, axis=1), "seq")
    dispatch = (raised / col_total[:, None]).astype(jnp.bfloat16)
    gathered_in = jnp.dot(dispatch, tokens_local, preferred_element_type=jnp.float32)
    gathered_back = jnp.dot(combine_low, grads_local, preferred_element_type=jnp.float32)
    slot_both = lax.psum_scatter(
        jnp.concatenate([gathered_in, gathered_back], axis=1),
        "seq",
        scatter_dimension=0,
        tiled=True,
    )
    slot_sum = slot_both[:, :width]
    slot_in = slot_sum.astype(jnp.bfloat16)
    slot_back = slot_both[:, width:].astype(jnp.bfloat16)
    clips = lax.axis_size("dp")
    every_in, every_back = (
        lax.all_gather(slot_in, "dp", axis=0, tiled=True),
        lax.all_gather(slot_back, "dp", axis=0, tiled=True),
    )
    every_in = every_in.reshape(clips, owned, width)
    every_back = every_back.reshape(clips, owned, width)
    hidden_pre = jnp.einsum("ced,edf->cef", every_in, w_in, preferred_element_type=jnp.float32)
    activated_f, gelu_back = jax.vjp(jax.nn.gelu, hidden_pre)
    activated = activated_f.astype(jnp.bfloat16)
    out_part = jnp.einsum("cef,efd->ced", activated, w_out, preferred_element_type=jnp.float32)
    act_back = jnp.einsum("ced,efd->cef", every_back, w_out, preferred_element_type=jnp.float32)
    hidden_back = gelu_back(act_back)[0].astype(jnp.bfloat16)
    w_out_grad = jnp.einsum(
        "cef,ced->efd", activated, every_back, preferred_element_type=jnp.float32
    ).astype(jnp.bfloat16)
    w_in_grad = jnp.einsum(
        "ced,cef->edf", every_in, hidden_back, preferred_element_type=jnp.float32
    ).astype(jnp.bfloat16)
    in_part = jnp.einsum("cef,edf->ced", hidden_back, w_in, preferred_element_type=jnp.float32)
    out_sum, in_sum = (
        lax.psum_scatter(out_part, "dp", scatter_dimension=0, tiled=True),
        lax.psum_scatter(in_part, "dp", scatter_dimension=0, tiled=True),
    )
    slot_in_back = in_sum[0].astype(jnp.bfloat16)
    all_out, all_in_back = (
        lax.all_gather(out_sum[0].astype(jnp.bfloat16), "seq", axis=0, tiled=True),
        lax.all_gather(slot_in_back, "seq", axis=0, tiled=True),
    )
    combine_back = contract_last(all_out, grads_local)
    logit_comb = combine * (combine_back - jnp.sum(combine * combine_back, axis=0, keepdims=True))
    dispatch_back = contract_last(all_in_back, tokens_local)
    weights = dispatch.astype(jnp.float32)
    slot_total = lax.psum(jnp.sum(weights * dispatch_back, axis=1), "seq")
    logit_back = (logit_comb + weights * (dispatch_back - slot_total[:, None])).astype(jnp.bfloat16)
    router_part = jnp.dot(logit_back, tokens_local, preferred_element_type=jnp.float32)
    router_grad = lax.psum(router_part, ("dp", "seq")) / math.sqrt(clips)
    token_part = contract_first(dispatch, all_in_back) + contract_first(logit_back, router)
    token_grad = (token_part * 64.0).astype(jnp.bfloat16)[None]
    return (token_grad, router_grad, w_in_grad, w_out_grad)


def solution(mesh):
    return jax.shard_map(
        local,
        mesh=mesh,
        in_specs=(
            P("dp", "seq", None),
            P("dp", "seq", None),
            P("dp", None, "seq"),
            P(),
            P("seq", None, "dp"),
            P("seq", "dp", None),
        ),
        out_specs=(P("dp", "seq", None), P(), P("seq", None, "dp"), P("seq", "dp", None)),
        check_vma=False,
    )
```

profile of v0, /device:TPU:1, one launch (start us, length us, event | category | flops | bytes accessed | tf_op | source)
XLA Modules:
  0.0 1347.4 jit_solution(13119178931065816833)
XLA Ops:
  7.2 0.0 copy-start
  7.2 0.0 copy-start.3
  7.2 0.0 all-reduce.8.cloned.1.call-start
  7.2 0.9 fusion.66
  8.2 51.4 %pmax.7 = f32[16]{0:T(128)S(1)} all-reduce(f32[16]{0:T(128)S(1)} %get-tuple-element.7), channel_id=1, replica_groups=mesh['dp'=32,'seq'=16] {'seq'}, use_global_device_ids=true, to_apply=%region_1.0 | all-reduce | flops 16 | bytes 128 | tf_op jit(solution)/shard_map/pmax | solution.py:29
  59.5 0.9 fusion.58
  60.4 50.4 %psum.21 = f32[16]{0:T(128)S(1)} all-reduce(f32[16]{0:T(128)S(1)} %get-tuple-element.5), channel_id=1, replica_groups=mesh['dp'=32,'seq'=16] {'seq'}, use_global_device_ids=true, to_apply=%region_3.0 | all-reduce | flops 16 | bytes 128 | tf_op jit(solution)/shard_map/psum | solution.py:31
  110.8 1.3 fusion.7
  112.1 0.0 copy-done
  112.1 0.0 copy-start.2
  112.1 1.0 fusion.13
  113.2 82.5 %all-reduce.9 = bf16[16,2560]{1,0:T(8,128)(2,1)S(1)} all-reduce(f32[16,2560]{1,0:T(8,128)S(1)} %pad_maximum_fusion), channel_id=4, replica_groups=mesh['dp'=32,'seq'=16] {'seq'}, use_global_device_ids=true, to_apply=%region_6.0.clone | all-reduce | flops 40960 | bytes 245760
  195.7 1.3 dynamic-slice
  197.0 0.7 dynamic-slice_convert_fusion
  197.7 142.7 %all-gather.3 = bf16[32,1,1280]{2,1,0:T(2,128)(2,1)S(1)} all-gather(bf16[1,1,1280]{2,1,0:T(2,128)(2,1)S(1)} %get-tuple-element.14), channel_id=1, replica_groups=mesh['dp'=32,'seq'=16] {'dp'}, dimensions={0}, use_global_device_ids=true | all-gather | bytes 84480 | tf_op jit(solution)/shard_map/all_gather | solution.py:46
  340.4 132.1 %all-gather.2 = bf16[32,1,1280]{2,1,0:T(2,128)(2,1)S(1)} all-gather(bf16[1,1,1280]{2,1,0:T(2,128)(2,1)S(1)} %get-tuple-element.13), channel_id=1, replica_groups=mesh['dp'=32,'seq'=16] {'dp'}, dimensions={0}, use_global_device_ids=true | all-gather | bytes 84480 | tf_op jit(solution)/shard_map/all_gather | solution.py:47
  472.5 0.0 copy-done.3
  472.5 0.0 copy-start.1
  472.5 0.2 convolution_bitcast_fusion.2
  472.7 0.0 copy-done.2
  472.7 0.2 convolution_bitcast_fusion
  473.0 0.0 copy-start.4
  473.0 0.3 fusion.39
  473.3 0.2 convolution_bitcast_fusion.1
  473.4 1.3 dynamic-slice.2
  474.7 268.7 %all-reduce.10 = (bf16[32,1,1280]{2,0,1:T(8,128)(2,1)S(1)}, bf16[32,1,1280]{2,0,1:T(8,128)(2,1)S(1)}) all-reduce(f32[32,1,1280]{2,0,1:T(8,128)S(1)} %convolution_bitcast_fusion.1, f32[32,1,1280]{2,0,1:T(8,128)S(1)} %convolution_bitcast_fusion), channel_id=5, replica_groups=mesh['dp'=32,'seq'=16] {'dp'}, use_global_device_ids=true, to_apply=%region_7.0.clone | all-reduce | flops 81920 | bytes 491520
  743.4 0.7 fusion.64
  744.1 89.9 %all-gather.1 = bf16[16,1,1280]{2,1,0:T(2,128)(2,1)S(1)} all-gather(bf16[1,1,1280]{2,1,0:T(2,128)(2,1)S(1)} %fusion.64), channel_id=3, replica_groups=mesh['dp'=32,'seq'=16] {'seq'}, dimensions={0}, use_global_device_ids=true | all-gather | bytes 43520 | tf_op jit(solution)/shard_map/all_gather | solution.py:70
  834.0 0.0 copy-done.1
  834.0 0.2 fusion.5
  834.2 0.7 fusion.65
  835.0 27.2 %all-gather = bf16[16,1,1280]{2,1,0:T(2,128)(2,1)S(1)} all-gather(bf16[1,1,1280]{2,1,0:T(2,128)(2,1)S(1)} %fusion.65), channel_id=2, replica_groups=mesh['dp'=32,'seq'=16] {'seq'}, dimensions={0}, use_global_device_ids=true | all-gather | bytes 43520 | tf_op jit(solution)/shard_map/all_gather | solution.py:71
  862.2 0.0 copy-done.4
  862.2 0.4 fusion.48
  862.6 44.6 %psum.22 = f32[16]{0:T(128)S(1)} all-reduce(f32[16]{0:T(128)S(1)} %get-tuple-element.10), channel_id=1, replica_groups=mesh['dp'=32,'seq'=16] {'seq'}, use_global_device_ids=true, to_apply=%region_11.0 | all-reduce | flops 16 | bytes 128 | tf_op jit(solution)/shard_map/psum | solution.py:77
  907.3 0.1 fusion.50
  907.3 0.0 copy-start.5
  907.3 0.9 fusion.9
  908.2 0.0 all-reduce.8.cloned.1.call-update
  908.2 0.4 fusion.26
  908.6 1.1 fusion.4
  909.6 0.0 copy-done.5
  909.6 1.2 fusion.2
  910.8 1.1 fusion.3
  911.9 427.2 %all-reduce.8.cloned.1.call-done = f32[16,1280]{1,0:T(8,128)} async-done(((f32[16,1280]{1,0:T(8,128)}), f32[16,1280]{1,0:T(8,128)}) %all-reduce.8.cloned.1.call-update) | async-done | bytes 81936 | tf_op jit(solution)/shard_map/psum | solution.py:80
  1339.1 1.5 broadcast_multiply_fusion
  (2 shorter events, 0.0 us)
Async XLA Ops:
  7.2 105.0 %copy-start = (bf16[1,256,1280]{2,1,0:T(8,128)(2,1)S(1)}, bf16[1,256,1280]{2,1,0:T(8,128)(2,1)}, u32[]{:S(2)}) copy-start(bf16[1,256,1280]{2,1,0:T(8,128)(2,1)} %param.6) | copy-start | bytes 1966084
  7.2 465.3 %copy-start.3 = (bf16[1,1280,160]{1,2,0:T(8,128)(2,1)S(1)}, bf16[1,1280,160]{1,2,0:T(8,128)(2,1)}, u32[]{:S(2)}) copy-start(bf16[1,1280,160]{1,2,0:T(8,128)(2,1)} %param.10) | copy-start | bytes 1228804
  7.2 1331.9 %all-reduce.8.cloned.1.call-start = ((), (), s32[]{:S(2)}) async-start(), calls=%async_computation | async-start | bytes 163840 | tf_op jit(solution)/shard_map/psum | solution.py:80
  112.1 360.6 %copy-start.2 = (bf16[1,160,1280]{2,1,0:T(8,128)(2,1)S(1)}, bf16[1,160,1280]{2,1,0:T(8,128)(2,1)}, u32[]{:S(2)}) copy-start(bf16[1,160,1280]{2,1,0:T(8,128)(2,1)} %param.11) | copy-start | bytes 1228804
  472.5 361.5 %copy-start.1 = (bf16[1,256,1280]{2,1,0:T(8,128)(2,1)S(1)}, bf16[1,256,1280]{2,1,0:T(8,128)(2,1)}, u32[]{:S(2)}) copy-start(bf16[1,256,1280]{2,1,0:T(8,128)(2,1)} %param.7) | copy-start | bytes 1966084
  473.0 389.2 %copy-start.4 = (f32[1,16,256]{2,1,0:T(8,128)S(1)}, f32[1,16,256]{2,1,0:T(8,128)}, u32[]{:S(2)}) copy-start(f32[1,16,256]{2,1,0:T(8,128)} %param.8) | copy-start | bytes 49156
  907.3 2.3 copy-start.5
Sparse Core Ops, SparseCore 0:
  908.3 430.6 all-reduce.7
where the time goes:
time: 1350 us
  blocking collectives  890 us (66%)
  waiting for transfers between devices  427 us (32%)
  between operations  14.2 us (1%)
    psum x1, waiting for transfers between devices, local(): router_grad = lax.psum(router_part, ('dp', 'seq')) / math.sqrt(clips)  427 us
    unnamed x2, blocking collectives  351 us
    all_gather x1, blocking collectives, local(): lax.all_gather(slot_in, 'dp', axis=0, tiled=True)  143 us
    all_gather x1, blocking collectives, local(): lax.all_gather(slot_back, 'dp', axis=0, tiled=True)  132 us
    all_gather x1, blocking collectives, local(): lax.all_gather(out_sum[0].astype(jnp.bfloat16), 'seq', axis=0, tiled=True)  89.9 us
    pmax x1, blocking collectives, local(): col_peak = lax.pmax(jnp.max(logit_rows, axis=1), 'seq')  51.4 us
    psum x1, blocking collectives, local(): col_total = lax.psum(jnp.sum(raised, axis=1), 'seq')  50.4 us
    psum x1, blocking collectives, local(): slot_total = lax.psum(jnp.sum(weights * dispatch_back, axis=1), 'seq')  44.6 us
  transfers between devices with their start and end apart: 1, of which 1 were waited for; matrix products, arithmetic and copies ran while one was open for 0% of the time, Pallas kernels for 0%

commit v1 on v0

v1 whole, which is shorter than its diff:
```python
import functools
import math

import jax
import jax.numpy as jnp
from jax import lax
from jax.experimental import pallas as pl
from jax.experimental.pallas import tpu as pltpu
from jax.sharding import PartitionSpec as P

MESH = pl.DeviceIdType.MESH
F32 = jnp.float32
BF16 = jnp.bfloat16

D = 1280
CH = D // 128
REC = 24
ZN = 16
XYN = 16
Z_ORDER = (8, 7, 9, 6, 10, 5, 11, 4, 12, 3, 13, 2, 14, 1, 15)
XY_ORDER = (
    (2, 2), (2, 1), (2, 3), (1, 2), (3, 2), (1, 1), (1, 3), (3, 1), (3, 3), (2, 0), (0, 2), (1, 0), (3, 0), (0, 1), (0, 3),
)


def low(value):
    return value.astype(BF16).astype(F32)


def dot(left, right, dims):
    return lax.dot_general(left, right, (dims, ((), ())), preferred_element_type=F32)


def kernel(
    tokens_hbm, grads_hbm, logits_hbm, router_hbm, w_in_hbm, w_out_hbm,
    token_grad_hbm, router_grad_ref, w_in_grad_hbm, w_out_grad_hbm,
    tokens_v, grads_v, logits_v, router_v, w_in_v, w_out_v, token_grad_v, w_in_grad_v, w_out_grad_v,
    sa, ra, sz, rz, sb, rb, wide, sc, rc, sd, rd, se, sf, rf, sg, rg, sh, rh, ri,
    in_sem, out_sem, send_sem, recv_sem,
):
    dp, sq = lax.axis_index("dp"), lax.axis_index("seq")
    zhi, xy = dp // 16, lax.rem(dp, 16)
    zlo, core = sq // 2, lax.rem(sq, 2)
    z = zhi * 8 + zlo
    x, y = xy // 4, lax.rem(xy, 4)

    def device(z_to, xy_to, core_to):
        return (z_to // 8 * 16 + xy_to, lax.rem(z_to, 8) * 2 + core_to)

    z_peers = [lax.rem(z + k, ZN) for k in Z_ORDER]
    xy_peers = [lax.rem(x + dx, 4) * 4 + lax.rem(y + dy, 4) for dx, dy in XY_ORDER]
    sibling = device(z, xy, 1 - core)

    loads = []
    for i, (src, dst) in enumerate(
        (
            (logits_hbm, logits_v),
            (tokens_hbm, tokens_v),
            (grads_hbm, grads_v),
            (router_hbm, router_v),
            (w_in_hbm, w_in_v),
            (w_out_hbm, w_out_v),
        )
    ):
        copy = pltpu.make_async_copy(src, dst, in_sem.at[i])
        copy.start()
        loads.append(copy)

    barrier = pltpu.get_barrier_semaphore()
    for z_to in z_peers:
        pl.semaphore_signal(barrier, inc=1, device_id=device(z_to, xy, core), device_id_type=MESH)
    for xy_to in xy_peers:
        pl.semaphore_signal(barrier, inc=1, device_id=device(z, xy_to, core), device_id_type=MESH)
    pl.semaphore_signal(barrier, inc=1, device_id=sibling, device_id_type=MESH)

    def send(stage, src, dst, to):
        pltpu.make_async_remote_copy(
            src_ref=src,
            dst_ref=dst,
            send_sem=send_sem.at[stage],
            recv_sem=recv_sem.at[stage],
            device_id=to,
            device_id_type=MESH,
        ).start()

    def wait(sem, ref):
        pltpu.make_async_copy(ref, ref, sem).wait()

    row = lax.broadcasted_iota(jnp.int32, (REC, 128), 0)
    lane = lax.broadcasted_iota(jnp.int32, (REC, 128), 1)

    def chunk(value, j):
        return value[:, j * 128 : (j + 1) * 128]

    def core_major(rows):
        return jnp.concatenate([rows[2 * j + p : 2 * j + p + 1] for p in range(2) for j in range(8)], axis=0)

    loads[0].wait()
    logits = core_major(logits_v[0])
    raised_c = jnp.exp(logits - jnp.max(logits, axis=0, keepdims=True))
    combine = raised_c / jnp.sum(raised_c, axis=0, keepdims=True)
    peak = low(jnp.max(logits, axis=1, keepdims=True))
    raised = jnp.exp(logits - peak)
    total = jnp.sum(raised, axis=1, keepdims=True)
    loads[1].wait()
    gathered = dot(raised.astype(BF16), tokens_v[0], ((1,), (0,)))
    loads[2].wait()
    backs = dot(combine.astype(BF16), grads_v[0], ((1,), (0,)))
    for j in range(CH):
        sa[pl.ds(j, 16, stride=REC), :] = chunk(gathered, j)
        sa[pl.ds(CH + j, 16, stride=REC), :] = chunk(backs, j)
    sa[pl.ds(20, 16, stride=REC), :] = jnp.broadcast_to(peak, (16, 128))
    sa[pl.ds(21, 16, stride=REC), :] = jnp.broadcast_to(total, (16, 128))
    for i in (22, 23):
        sa[pl.ds(i, 16, stride=REC), :] = jnp.zeros((16, 128), F32)
    loads[3].wait()
    router = core_major(router_v[...].astype(F32))
    loads[4].wait()
    loads[5].wait()

    pl.semaphore_wait(barrier, 31)

    send(0, sa.at[pl.ds((1 - core) * 192, 192)], ra, sibling)
    wait(recv_sem.at[0], ra)
    own = sa[pl.ds(pl.multiple_of(core * 192, 192), 192), :].reshape(8, REC, 128)
    other = ra[...].reshape(8, REC, 128)
    scaled = (row < CH) | (row == 21)
    top = jnp.maximum(own[:, 20:21, :], other[:, 20:21, :])
    both = own * jnp.where(scaled, jnp.exp(own[:, 20:21, :] - top), 1.0) + other * jnp.where(
        scaled, jnp.exp(other[:, 20:21, :] - top), 1.0
    )
    count = both[:, 21:22, :]
    both = jnp.where(row == 20, top, jnp.where(row == 22, count - low(count), both))
    sz[...] = both.astype(BF16)
    rz[pl.ds(z, 1)] = sz[pl.ds(zlo, 1)]

    for z_to in z_peers:
        send(1, sz.at[lax.rem(z_to, 8)], rz.at[z], device(z_to, xy, core))
    wait(recv_sem.at[1], rz.at[pl.ds(0, ZN - 1)])
    slots, tops, totals = [], [], []
    for h in range(2):
        part = rz[pl.ds(8 * h, 8)].astype(F32)
        peaks = part[:, 20:21, :]
        top = jnp.max(peaks, axis=0)
        factor = jnp.exp(peaks - top)
        count = jnp.sum(factor * (part[:, 21:22, :] + part[:, 22:23, :]), axis=0)
        summed = jnp.sum(part * jnp.where(row < CH, factor, 1.0), axis=0)
        slots.append(jnp.where(row < CH, summed / count, summed))
        tops.append(top)
        totals.append(count)
        sb[pl.ds(REC * h, REC), :] = slots[h]
    packed = sb[...].astype(BF16)
    rb[pl.ds(xy, 1)] = packed[None]

    for xy_to in xy_peers:
        send(2, rb.at[xy], rb.at[xy], device(z, xy_to, core))
    wait(recv_sem.at[2], rb.at[pl.ds(0, XYN - 1)])
    wide[...] = rb[...].astype(F32).reshape(XYN * 48, 128)

    def clips(first):
        return jnp.concatenate(
            [
                jnp.concatenate(
                    [wide[pl.ds(h * REC + first + j, 16, stride=48), :].astype(BF16) for j in range(CH)],
                    axis=1,
                )
                for h in range(2)
            ],
            axis=0,
        )

    every_in, every_back = clips(0), clips(CH)
    pre = dot(every_in, w_in_v[0], ((1,), (0,)))
    act_back = dot(every_back, w_out_v[0], ((1,), (1,)))
    slope = math.sqrt(2.0 / math.pi)
    bent = jnp.tanh(slope * (pre + 0.044715 * (pre * pre * pre)))
    activated = (0.5 * pre * (1.0 + bent)).astype(BF16)
    gelu_slope = 0.5 * (1.0 + bent) + 0.5 * pre * ((1.0 + bent) * (1.0 - bent)) * (
        slope * (1.0 + 3.0 * 0.044715 * (pre * pre))
    )
    hidden_back = (gelu_slope * act_back).astype(BF16)
    in_part = dot(hidden_back, w_in_v[0], ((1,), (1,)))
    out_part = dot(activated, w_out_v[0], ((1,), (0,)))
    for h in range(2):
        for j in range(CH):
            wide[pl.ds(h * REC + j, 16, stride=48), :] = chunk(in_part, j)[16 * h : 16 * h + 16]
            wide[pl.ds(h * REC + CH + j, 16, stride=48), :] = chunk(out_part, j)[16 * h : 16 * h + 16]
    sc[...] = wide[...].reshape(XYN, 48, 128).astype(BF16)
    rc[pl.ds(xy, 1)] = sc[pl.ds(xy, 1)]

    for xy_to in xy_peers:
        send(3, sc.at[xy_to], rc.at[xy], device(z, xy_to, core))
    w_out_grad_v[0] = dot(activated, every_back, ((0,), (0,))).astype(BF16)
    w_in_grad_v[0] = dot(every_in, hidden_back, ((0,), (0,))).astype(BF16)
    stores = [
        pltpu.make_async_copy(w_in_grad_v, w_in_grad_hbm, out_sem.at[0]),
        pltpu.make_async_copy(w_out_grad_v, w_out_grad_hbm, out_sem.at[1]),
        pltpu.make_async_copy(token_grad_v, token_grad_hbm, out_sem.at[2]),
    ]
    stores[0].start()
    stores[1].start()
    wait(recv_sem.at[3], rc.at[pl.ds(0, XYN - 1)])
    halves = jnp.sum(rc[...].astype(F32), axis=0)
    for h in range(2):
        half = halves[REC * h : REC * h + REC]
        dotted = jnp.sum(jnp.where(row < CH, low(half) * slots[h], 0.0), keepdims=True)
        half = jnp.where(row == 20, tops[h], half)
        half = jnp.where(row == 21, totals[h], half)
        half = jnp.where(row == 22, totals[h] - low(totals[h]), half)
        half = jnp.where(row == 23, jnp.where(lane < 64, dotted, dotted - low(dotted)), half)
        sd[pl.ds(h, 1)] = half.astype(BF16)[None]
    rd[pl.ds(z, 1)] = sd[pl.ds(zhi, 1)]

    for z_to in z_peers:
        send(4, sd.at[z_to // 8], rd.at[z], device(z_to, xy, core))
    wait(recv_sem.at[4], rd.at[pl.ds(0, ZN - 1)])
    first, second = rd[pl.ds(0, 8)].astype(F32), rd[pl.ds(8, 8)].astype(F32)
    both = first + second
    dotted = both[:, 23:24, 0:1] + both[:, 23:24, 64:65]
    both = jnp.where(row == 20, first, both)
    both = jnp.where(row == 21, first[:, 21:22, :] + first[:, 22:23, :], both)
    both = jnp.where(row == 23, dotted, both)
    mine = pl.ds(pl.multiple_of(core * 192, 192), 192)
    se[mine, :] = both.reshape(192, 128)

    send(5, se.at[mine], se.at[mine], sibling)
    wait(recv_sem.at[5], ra)

    def slot_rows(first):
        return jnp.concatenate([se[pl.ds(first + j, 16, stride=REC), :] for j in range(CH)], axis=1).astype(BF16)

    in_back, slot_out = slot_rows(0), slot_rows(CH)
    col_peak = se[pl.ds(20, 16, stride=REC), :][:, 0:1]
    col_total = se[pl.ds(21, 16, stride=REC), :][:, 0:1]
    slot_total = se[pl.ds(23, 16, stride=REC), :][:, 0:1]
    dispatch = (jnp.exp(logits - col_peak) / col_total).astype(BF16)
    weights = dispatch.astype(F32)
    combine_back = dot(slot_out, grads_v[0], ((1,), (1,)))
    dispatch_back = dot(in_back, tokens_v[0], ((1,), (1,)))
    logit_comb = combine * (combine_back - jnp.sum(combine * combine_back, axis=0, keepdims=True))
    logit_back = (logit_comb + weights * (dispatch_back - slot_total)).astype(BF16)
    router_part = dot(logit_back, tokens_v[0], ((1,), (0,)))
    for j in range(CH):
        ri[pl.ds(j, 16, stride=16), :] = chunk(router_part, j)
    for j in range(CH, 16):
        ri[pl.ds(j, 16, stride=16), :] = jnp.zeros((16, 128), F32)
    sf[...] = ri[...].reshape(16, 16, 128).astype(BF16)
    rf[pl.ds(xy, 1)] = sf[pl.ds(xy, 1)]

    for xy_to in xy_peers:
        send(6, sf.at[xy_to], rf.at[xy], device(z, xy_to, core))
    left = jnp.concatenate([weights, logit_back.astype(F32)], axis=0).astype(BF16)
    right = jnp.concatenate([in_back.astype(F32), router], axis=0).astype(BF16)
    token_grad_v[0] = (dot(left, right, ((0,), (0,))) * 64.0).astype(BF16)
    stores[2].start()
    wait(recv_sem.at[6], rf.at[pl.ds(0, XYN - 1)])
    sg[...] = jnp.sum(rf[...].astype(F32), axis=0)

    send(7, sg, rg, sibling)
    wait(recv_sem.at[7], rg)
    sh[...] = (sg[...] + rg[...]).astype(BF16)
    rh[pl.ds(z, 1)] = sh[...][None]
    for z_to in z_peers:
        send(8, sh, rh.at[z], device(z_to, xy, core))
    wait(recv_sem.at[8], rh.at[pl.ds(0, ZN - 1)])
    mine = pl.ds(pl.multiple_of((lax.rem(xy, 8) * 2 + xy // 8) * 16, 16), 16)
    ri[mine, :] = jnp.sum(rh[...].astype(F32), axis=0) / math.sqrt(32.0)

    for xy_to in xy_peers:
        send(9, ri.at[mine], ri.at[mine], device(z, xy_to, core))
    wait(recv_sem.at[9], ri.at[pl.ds(0, 240)])
    for j in range(CH):
        router_grad_ref[:, j * 128 : (j + 1) * 128] = ri[pl.ds(j, 16, stride=16), :]

    wait(send_sem.at[0], ra)
    wait(send_sem.at[1], rz.at[pl.ds(0, ZN - 1)])
    wait(send_sem.at[2], rb.at[pl.ds(0, XYN - 1)])
    wait(send_sem.at[3], rc.at[pl.ds(0, XYN - 1)])
    wait(send_sem.at[4], rd.at[pl.ds(0, ZN - 1)])
    wait(send_sem.at[5], ra)
    wait(send_sem.at[6], rf.at[pl.ds(0, XYN - 1)])
    wait(send_sem.at[7], rg)
    wait(send_sem.at[8], rh.at[pl.ds(0, ZN - 1)])
    wait(send_sem.at[9], ri.at[pl.ds(0, 240)])
    for copy in stores:
        copy.wait()


def local(tokens, out_grad, logits, router, w_in, w_out):
    hbm = pl.BlockSpec(memory_space=pl.ANY)
    inputs = (tokens, out_grad, logits, router, w_in, w_out)
    return pl.pallas_call(
        kernel,
        name="moe_back",
        out_shape=(
            jax.ShapeDtypeStruct(tokens.shape, BF16),
            jax.ShapeDtypeStruct(router.shape, F32),
            jax.ShapeDtypeStruct(w_in.shape, BF16),
            jax.ShapeDtypeStruct(w_out.shape, BF16),
        ),
        in_specs=[hbm] * 6,
        out_specs=(hbm, pl.BlockSpec(memory_space=pltpu.VMEM), hbm, hbm),
        scratch_shapes=[pltpu.VMEM(a.shape, a.dtype) for a in inputs]
        + [
            pltpu.VMEM(tokens.shape, BF16),
            pltpu.VMEM(w_in.shape, BF16),
            pltpu.VMEM(w_out.shape, BF16),
            pltpu.VMEM((16 * REC, 128), F32),
            pltpu.VMEM((8 * REC, 128), F32),
            pltpu.VMEM((8, REC, 128), BF16),
            pltpu.VMEM((ZN, REC, 128), BF16),
            pltpu.VMEM((2 * REC, 128), F32),
            pltpu.VMEM((XYN, 48, 128), BF16),
            pltpu.VMEM((XYN * 48, 128), F32),
            pltpu.VMEM((XYN, 48, 128), BF16),
            pltpu.VMEM((XYN, 48, 128), BF16),
            pltpu.VMEM((2, REC, 128), BF16),
            pltpu.VMEM((ZN, REC, 128), BF16),
            pltpu.VMEM((16 * REC, 128), F32),
            pltpu.VMEM((16, 16, 128), BF16),
            pltpu.VMEM((XYN, 16, 128), BF16),
            pltpu.VMEM((16, 128), F32),
            pltpu.VMEM((16, 128), F32),
            pltpu.VMEM((16, 128), BF16),
            pltpu.VMEM((ZN, 16, 128), BF16),
            pltpu.VMEM((16 * 16, 128), F32),
            pltpu.SemaphoreType.DMA((6,)),
            pltpu.SemaphoreType.DMA((3,)),
            pltpu.SemaphoreType.DMA((10,)),
            pltpu.SemaphoreType.DMA((10,)),
        ],
        compiler_params=pltpu.CompilerParams(
            collective_id=0, has_side_effects=True, vmem_limit_bytes=48 * 1024 * 1024
        ),
    )(*inputs)


def solution(mesh):
    return jax.shard_map(
        local,
        mesh=mesh,
        in_specs=(
            P("dp", "seq", None),
            P("dp", "seq", None),
            P("dp", None, "seq"),
            P(),
            P("seq", None, "dp"),
            P("seq", "dp", None),
        ),
        out_specs=(P("dp", "seq", None), P(), P("seq", None, "dp"), P("seq", "dp", None)),
        check_vma=False,
    )
```

time: 1350 us -> 70.4 us (0.05)
  blocking collectives: 890 us -> 0 us
  waiting for transfers between devices: 427 us -> 0 us
  Pallas kernels: 0 us -> 62.1 us
  between operations: 14.2 us -> 0.69 us
    psum x1 -> x0, waiting for transfers between devices: 427 us -> none  [local(): router_grad = lax.psum(router_part, ('dp', 'seq')) / math.sqrt(clips)]
    all_gather x4 -> x0, blocking collectives: 392 us -> none  [the longest x1 143 us: local(): lax.all_gather(slot_in, 'dp', axis=0, tiled=True)]
    unnamed x2 -> x0, blocking collectives: 351 us -> none
    psum x2 -> x0, blocking collectives: 95 us -> none  [the longest x1 50.4 us: local(): col_total = lax.psum(jnp.sum(raised, axis=1), 'seq')]
    pallas_call x0 -> x1, Pallas kernels: none -> 62.1 us  [local(): pl.pallas_call(kernel, name='moe_back', out_shape=(jax.ShapeDtypeStruct(t...]
    pmax x1 -> x0, blocking collectives: 51.4 us -> none  [local(): col_peak = lax.pmax(jnp.max(logit_rows, axis=1), 'seq')]
  transfers between devices with their start and end apart: 1 -> 0, of which waited for: 1 -> 0; matrix products, arithmetic and copies ran while one was open for 0% -> 0% of each run, Pallas kernels for 0% -> 0%
where the time goes in v1:
time: 70.4 us; the launch traced here: 69.8 us
  Pallas kernels  62.1 us (88%)
  local copies, waits for them, and re-layouts  7.1 us (10%)
    pallas_call x1, Pallas kernels, local(): pl.pallas_call(kernel, name='moe_back', out_shape=(jax.ShapeDtypeStruct(t...  62.1 us
    unnamed x14, local copies, waits for them, and re-layouts  6.13 us

profile of v1, /device:TPU:1, one launch (start us, length us, event | category | flops | bytes accessed | tf_op | source)
XLA Modules:
  0.0 69.8 jit_solution(2840948386403716900)
XLA Ops:
  0.6 0.0 copy-start.2
  0.6 0.0 copy-start
  0.7 1.3 %copy.10.w_in_hbm = bf16[1,1280,160]{2,1,0:T(8,128)(2,1)S(1)} copy(bf16[1,1280,160]{1,2,0:T(8,128)(2,1)} %param.10) | data formatting | bytes 819200 | tf_op args[4]
  2.0 0.0 copy-done.2
  2.0 0.0 copy-done
  2.0 0.0 copy-start.1
  2.0 1.1 %copy-done.1 = bf16[1,256,1280]{2,1,0:T(8,128)(2,1)S(1)} copy-done((bf16[1,256,1280]{2,1,0:T(8,128)(2,1)S(1)}, bf16[1,256,1280]{2,1,0:T(8,128)(2,1)}, u32[]{:S(2)}) %copy-start.1) | copy-done | bytes 655384
  3.1 0.0 copy-start.3
  3.1 0.8 %copy-done.3 = bf16[16,1280]{1,0:T(8,128)(2,1)S(1)} copy-done((bf16[16,1280]{1,0:T(8,128)(2,1)S(1)}, bf16[16,1280]{1,0:T(8,128)(2,1)}, u32[]{:S(2)}) %copy-start.3) | copy-done | bytes 40984
  3.9 0.0 copy-start.4
  3.9 0.7 %copy-done.4 = f32[1,16,256]{2,1,0:T(8,128)S(1)} copy-done((f32[1,16,256]{2,1,0:T(8,128)S(1)}, f32[1,16,256]{2,1,0:T(8,128)}, u32[]{:S(2)}) %copy-start.4) | copy-done | bytes 16408
  4.6 62.1 %moe_back.1 = (bf16[1,256,1280]{2,1,0:T(8,128)(2,1)S(1)}, f32[16,1280]{1,0:T(8,128)S(1)}, bf16[1,1280,160]{2,1,0:T(8,128)(2,1)S(1)}, bf16[1,160,1280]{2,1,0:T(8,128)(2,1)S(1)}) custom-call(bf16[1,256,1280]{2,1,0:T(8,128)(2,1)S(1)} %copy-done, bf16[1,256,1280]{2,1,0:T(8,128)(2,1)S(1)} %copy-done.1, f32[1,16,256]{2,1,0:T(8,128)S(1)} %copy-done.4, ...), custom_call_target="tpu_custom_call" | custom-call | tf_op jit(solution)/shard_map/moe_back/pallas_call | solution.py:292
  66.6 1.0 %copy.11 = bf16[1,1280,160]{1,2,0:T(8,128)(2,1)} copy(bf16[1,1280,160]{2,1,0:T(8,128)(2,1)S(1)} %get-tuple-element.6) | data formatting | bytes 819200 | tf_op jit(solution)/shard_map/moe_back/pallas_call | solution.py:292
  67.6 0.8 %copy.15 = bf16[1,256,1280]{2,1,0:T(8,128)(2,1)} copy(bf16[1,256,1280]{2,1,0:T(8,128)(2,1)S(1)} %get-tuple-element.12) | data formatting | bytes 1310720
  68.5 0.6 copy.16
  69.1 0.8 %copy.17 = bf16[1,160,1280]{2,1,0:T(8,128)(2,1)} copy(bf16[1,160,1280]{2,1,0:T(8,128)(2,1)S(1)} %get-tuple-element.15) | data formatting | bytes 819200
Async XLA Ops:
  0.6 1.4 %copy-start.2 = (bf16[1,160,1280]{2,1,0:T(8,128)(2,1)S(1)}, bf16[1,160,1280]{2,1,0:T(8,128)(2,1)}, u32[]{:S(2)}) copy-start(bf16[1,160,1280]{2,1,0:T(8,128)(2,1)} %w_out_hbm.1) | copy-start | bytes 1228804
  0.6 1.4 %copy-start = (bf16[1,256,1280]{2,1,0:T(8,128)(2,1)S(1)}, bf16[1,256,1280]{2,1,0:T(8,128)(2,1)}, u32[]{:S(2)}) copy-start(bf16[1,256,1280]{2,1,0:T(8,128)(2,1)} %tokens_hbm.1) | copy-start | bytes 1966084
  2.0 1.1 %copy-start.1 = (bf16[1,256,1280]{2,1,0:T(8,128)(2,1)S(1)}, bf16[1,256,1280]{2,1,0:T(8,128)(2,1)}, u32[]{:S(2)}) copy-start(bf16[1,256,1280]{2,1,0:T(8,128)(2,1)} %grads_hbm.1) | copy-start | bytes 1966084
  3.1 0.8 %copy-start.3 = (bf16[16,1280]{1,0:T(8,128)(2,1)S(1)}, bf16[16,1280]{1,0:T(8,128)(2,1)}, u32[]{:S(2)}) copy-start(bf16[16,1280]{1,0:T(8,128)(2,1)} %router_hbm.1) | copy-start | bytes 122884
  3.9 0.7 %copy-start.4 = (f32[1,16,256]{2,1,0:T(8,128)S(1)}, f32[1,16,256]{2,1,0:T(8,128)}, u32[]{:S(2)}) copy-start(f32[1,16,256]{2,1,0:T(8,128)} %logits_hbm.1) | copy-start | bytes 49156

commit v2 on v1

--- a/solution.py
+++ b/solution.py
@@ -14,6 +14,7 @@
 
 D = 1280
 CH = D // 128
+PAIR = 4 * CH
 REC = 24
 ZN = 16
 XYN = 16
@@ -33,9 +34,9 @@
 
 def kernel(
     tokens_hbm, grads_hbm, logits_hbm, router_hbm, w_in_hbm, w_out_hbm,
-    token_grad_hbm, router_grad_ref, w_in_grad_hbm, w_out_grad_hbm,
-    tokens_v, grads_v, logits_v, router_v, w_in_v, w_out_v, token_grad_v, w_in_grad_v, w_out_grad_v,
-    sa, ra, sz, rz, sb, rb, wide, sc, rc, sd, rd, se, sf, rf, sg, rg, sh, rh, ri,
+    token_grad_hbm, router_grad_hbm, w_in_grad_hbm, w_out_grad_hbm,
+    tokens_v, grads_v, logits_v, router_v, w_in_v, w_out_v, token_grad_v, router_grad_ref, w_in_grad_v, w_out_grad_v,
+    sa, ra, sz, rz, sb, rb, wide, sc, rc, halves, sd, rd, se, rows, sf, rf, sh, rh, ri,
     in_sem, out_sem, send_sem, recv_sem,
 ):
     dp, sq = lax.axis_index("dp"), lax.axis_index("seq")
@@ -71,6 +72,8 @@
         pl.semaphore_signal(barrier, inc=1, device_id=device(z_to, xy, core), device_id_type=MESH)
     for xy_to in xy_peers:
         pl.semaphore_signal(barrier, inc=1, device_id=device(z, xy_to, core), device_id_type=MESH)
+    for xy_to in xy_peers:
+        pl.semaphore_signal(barrier, inc=1, device_id=device(z, xy_to, 1 - core), device_id_type=MESH)
     pl.semaphore_signal(barrier, inc=1, device_id=sibling, device_id_type=MESH)
 
     def send(stage, src, dst, to):
@@ -113,12 +116,13 @@
     sa[pl.ds(21, 16, stride=REC), :] = jnp.broadcast_to(total, (16, 128))
     for i in (22, 23):
         sa[pl.ds(i, 16, stride=REC), :] = jnp.zeros((16, 128), F32)
+    halves[pl.ds(PAIR, 8), :] = jnp.zeros((8, 128), F32)
     loads[3].wait()
     router = core_major(router_v[...].astype(F32))
     loads[4].wait()
     loads[5].wait()
 
-    pl.semaphore_wait(barrier, 31)
+    pl.semaphore_wait(barrier, 46)
 
     send(0, sa.at[pl.ds((1 - core) * 192, 192)], ra, sibling)
     wait(recv_sem.at[0], ra)
@@ -148,20 +152,20 @@
         slots.append(jnp.where(row < CH, summed / count, summed))
         tops.append(top)
         totals.append(count)
-        sb[pl.ds(REC * h, REC), :] = slots[h]
+        sb[pl.ds(2 * CH * h, 2 * CH), :] = slots[h][: 2 * CH]
     packed = sb[...].astype(BF16)
     rb[pl.ds(xy, 1)] = packed[None]
 
     for xy_to in xy_peers:
         send(2, rb.at[xy], rb.at[xy], device(z, xy_to, core))
     wait(recv_sem.at[2], rb.at[pl.ds(0, XYN - 1)])
-    wide[...] = rb[...].astype(F32).reshape(XYN * 48, 128)
+    wide[...] = rb[...].astype(F32).reshape(XYN * PAIR, 128)
 
     def clips(first):
         return jnp.concatenate(
             [
                 jnp.concatenate(
-                    [wide[pl.ds(h * REC + first + j, 16, stride=48), :].astype(BF16) for j in range(CH)],
+                    [wide[pl.ds(h * 2 * CH + first + j, 16, stride=PAIR), :].astype(BF16) for j in range(CH)],
                     axis=1,
                 )
                 for h in range(2)
@@ -170,7 +174,7 @@
         )
 
     every_in, every_back = clips(0), clips(CH)
-    pre = dot(every_in, w_in_v[0], ((1,), (0,)))
+    pre = dot(every_in, w_in_v[0], ((1,), (1,)))
     act_back = dot(every_back, w_out_v[0], ((1,), (1,)))
     slope = math.sqrt(2.0 / math.pi)
     bent = jnp.tanh(slope * (pre + 0.044715 * (pre * pre * pre)))
@@ -179,30 +183,31 @@
         slope * (1.0 + 3.0 * 0.044715 * (pre * pre))
     )
     hidden_back = (gelu_slope * act_back).astype(BF16)
-    in_part = dot(hidden_back, w_in_v[0], ((1,), (1,)))
+    in_part = dot(hidden_back, w_in_v[0], ((1,), (0,)))
     out_part = dot(activated, w_out_v[0], ((1,), (0,)))
     for h in range(2):
         for j in range(CH):
-            wide[pl.ds(h * REC + j, 16, stride=48), :] = chunk(in_part, j)[16 * h : 16 * h + 16]
-            wide[pl.ds(h * REC + CH + j, 16, stride=48), :] = chunk(out_part, j)[16 * h : 16 * h + 16]
-    sc[...] = wide[...].reshape(XYN, 48, 128).astype(BF16)
+            wide[pl.ds(h * 2 * CH + j, 16, stride=PAIR), :] = chunk(in_part, j)[16 * h : 16 * h + 16]
+            wide[pl.ds(h * 2 * CH + CH + j, 16, stride=PAIR), :] = chunk(out_part, j)[16 * h : 16 * h + 16]
+    sc[...] = wide[...].reshape(XYN, PAIR, 128).astype(BF16)
     rc[pl.ds(xy, 1)] = sc[pl.ds(xy, 1)]
 
     for xy_to in xy_peers:
         send(3, sc.at[xy_to], rc.at[xy], device(z, xy_to, core))
     w_out_grad_v[0] = dot(activated, every_back, ((0,), (0,))).astype(BF16)
-    w_in_grad_v[0] = dot(every_in, hidden_back, ((0,), (0,))).astype(BF16)
+    w_in_grad_v[0] = dot(hidden_back, every_in, ((0,), (0,))).astype(BF16)
     stores = [
         pltpu.make_async_copy(w_in_grad_v, w_in_grad_hbm, out_sem.at[0]),
         pltpu.make_async_copy(w_out_grad_v, w_out_grad_hbm, out_sem.at[1]),
         pltpu.make_async_copy(token_grad_v, token_grad_hbm, out_sem.at[2]),
+        pltpu.make_async_copy(router_grad_ref, router_grad_hbm, out_sem.at[3]),
     ]
     stores[0].start()
     stores[1].start()
     wait(recv_sem.at[3], rc.at[pl.ds(0, XYN - 1)])
-    halves = jnp.sum(rc[...].astype(F32), axis=0)
+    halves[pl.ds(0, PAIR), :] = jnp.sum(rc[...].astype(F32), axis=0)
     for h in range(2):
-        half = halves[REC * h : REC * h + REC]
+        half = halves[pl.ds(2 * CH * h, REC), :]
         dotted = jnp.sum(jnp.where(row < CH, low(half) * slots[h], 0.0), keepdims=True)
         half = jnp.where(row == 20, tops[h], half)
         half = jnp.where(row == 21, totals[h], half)
@@ -241,10 +246,10 @@
     logit_back = (logit_comb + weights * (dispatch_back - slot_total)).astype(BF16)
     router_part = dot(logit_back, tokens_v[0], ((1,), (0,)))
     for j in range(CH):
-        ri[pl.ds(j, 16, stride=16), :] = chunk(router_part, j)
+        rows[pl.ds(j, 16, stride=16), :] = chunk(router_part, j)
     for j in range(CH, 16):
-        ri[pl.ds(j, 16, stride=16), :] = jnp.zeros((16, 128), F32)
-    sf[...] = ri[...].reshape(16, 16, 128).astype(BF16)
+        rows[pl.ds(j, 16, stride=16), :] = jnp.zeros((16, 128), F32)
+    sf[...] = rows[...].reshape(16, 16, 128).astype(BF16)
     rf[pl.ds(xy, 1)] = sf[pl.ds(xy, 1)]
 
     for xy_to in xy_peers:
@@ -254,23 +259,24 @@
     token_grad_v[0] = (dot(left, right, ((0,), (0,))) * 64.0).astype(BF16)
     stores[2].start()
     wait(recv_sem.at[6], rf.at[pl.ds(0, XYN - 1)])
-    sg[...] = jnp.sum(rf[...].astype(F32), axis=0)
-
-    send(7, sg, rg, sibling)
-    wait(recv_sem.at[7], rg)
-    sh[...] = (sg[...] + rg[...]).astype(BF16)
+    sh[...] = jnp.sum(rf[...].astype(F32), axis=0).astype(BF16)
     rh[pl.ds(z, 1)] = sh[...][None]
+
     for z_to in z_peers:
-        send(8, sh, rh.at[z], device(z_to, xy, core))
-    wait(recv_sem.at[8], rh.at[pl.ds(0, ZN - 1)])
-    mine = pl.ds(pl.multiple_of((lax.rem(xy, 8) * 2 + xy // 8) * 16, 16), 16)
-    ri[mine, :] = jnp.sum(rh[...].astype(F32), axis=0) / math.sqrt(32.0)
-
-    for xy_to in xy_peers:
-        send(9, ri.at[mine], ri.at[mine], device(z, xy_to, core))
-    wait(recv_sem.at[9], ri.at[pl.ds(0, 240)])
+        send(7, sh, rh.at[z], device(z_to, xy, core))
+    wait(recv_sem.at[7], rh.at[pl.ds(0, ZN - 1)])
+    place = core * 16 + lax.rem(xy, 8) * 2 + xy // 8
+    ri[pl.ds(place, 1)] = jnp.sum(rh[...].astype(F32), axis=0).astype(BF16)[None]
+
+    for xy_to in xy_peers:
+        send(8, ri.at[place], ri.at[place], device(z, xy_to, core))
+        send(8, ri.at[place], ri.at[place], device(z, xy_to, 1 - core))
+    send(8, ri.at[place], ri.at[place], sibling)
+    wait(recv_sem.at[8], ri.at[pl.ds(0, 31)])
+    rows[...] = ((ri[pl.ds(0, 16)].astype(F32) + ri[pl.ds(16, 16)].astype(F32)) / math.sqrt(32.0)).reshape(256, 128)
     for j in range(CH):
-        router_grad_ref[:, j * 128 : (j + 1) * 128] = ri[pl.ds(j, 16, stride=16), :]
+        router_grad_ref[:, j * 128 : (j + 1) * 128] = rows[pl.ds(j, 16, stride=16), :]
+    stores[3].start()
 
     wait(send_sem.at[0], ra)
     wait(send_sem.at[1], rz.at[pl.ds(0, ZN - 1)])
@@ -279,60 +285,90 @@
     wait(send_sem.at[4], rd.at[pl.ds(0, ZN - 1)])
     wait(send_sem.at[5], ra)
     wait(send_sem.at[6], rf.at[pl.ds(0, XYN - 1)])
-    wait(send_sem.at[7], rg)
-    wait(send_sem.at[8], rh.at[pl.ds(0, ZN - 1)])
-    wait(send_sem.at[9], ri.at[pl.ds(0, 240)])
+    wait(send_sem.at[7], rh.at[pl.ds(0, ZN - 1)])
+    wait(send_sem.at[8], ri.at[pl.ds(0, 31)])
     for copy in stores:
         copy.wait()
 
 
+def store_kernel(*refs):
+    sources, targets, sems = refs[:4], refs[4:8], refs[8]
+    copies = []
+    for a, b in zip(sources, targets):
+        if len(a.shape) == 2:
+            parts = [(a, b)]
+        else:
+            cut = a.shape[1] // 2
+            parts = [(a.at[:, pl.ds(i * cut, cut)], b.at[:, pl.ds(i * cut, cut)]) for i in range(2)]
+        for part, to in parts:
+            copies.append(pltpu.make_async_copy(part, to, sems.at[len(copies)]))
+            copies[-1].start()
+    for copy in copies:
+        copy.wait()
+
+
 def local(tokens, out_grad, logits, router, w_in, w_out):
-    hbm = pl.BlockSpec(memory_space=pl.ANY)
-    inputs = (tokens, out_grad, logits, router, w_in, w_out)
-    return pl.pallas_call(
+    anywhere = pl.BlockSpec(memory_space=pl.ANY)
+    hbm = pl.BlockSpec(memory_space=pltpu.HBM)
+    w_in = jnp.swapaxes(w_in, 1, 2)
+    inputs = tuple(
+        pltpu.with_memory_space_constraint(a, pltpu.HBM) for a in (tokens, out_grad, logits, router, w_in, w_out)
+    )
+    results = (
+        jax.ShapeDtypeStruct(tokens.shape, BF16),
+        jax.ShapeDtypeStruct(router.shape, F32),
+        jax.ShapeDtypeStruct(w_in.shape, BF16),
+        jax.ShapeDtypeStruct(w_out.shape, BF16),
+    )
+    made = pl.pallas_call(
         kernel,
         name="moe_back",
-        out_shape=(
-            jax.ShapeDtypeStruct(tokens.shape, BF16),
-            jax.ShapeDtypeStruct(router.shape, F32),
-            jax.ShapeDtypeStruct(w_in.shape, BF16),
-            jax.ShapeDtypeStruct(w_out.shape, BF16),
-        ),
+        out_shape=tuple(pltpu.VMEM(a.shape, a.dtype) for a in results),
         in_specs=[hbm] * 6,
-        out_specs=(hbm, pl.BlockSpec(memory_space=pltpu.VMEM), hbm, hbm),
+        out_specs=(anywhere,) * 4,
         scratch_shapes=[pltpu.VMEM(a.shape, a.dtype) for a in inputs]
         + [
             pltpu.VMEM(tokens.shape, BF16),
+            pltpu.VMEM(router.shape, F32),
             pltpu.VMEM(w_in.shape, BF16),
             pltpu.VMEM(w_out.shape, BF16),
             pltpu.VMEM((16 * REC, 128), F32),
             pltpu.VMEM((8 * REC, 128), F32),
             pltpu.VMEM((8, REC, 128), BF16),
             pltpu.VMEM((ZN, REC, 128), BF16),
-            pltpu.VMEM((2 * REC, 128), F32),
-            pltpu.VMEM((XYN, 48, 128), BF16),
-            pltpu.VMEM((XYN * 48, 128), F32),
-            pltpu.VMEM((XYN, 48, 128), BF16),
-            pltpu.VMEM((XYN, 48, 128), BF16),
+            pltpu.VMEM((PAIR, 128), F32),
+            pltpu.VMEM((XYN, PAIR, 128), BF16),
+            pltpu.VMEM((XYN * PAIR, 128), F32),
+            pltpu.VMEM((XYN, PAIR, 128), BF16),
+            pltpu.VMEM((XYN, PAIR, 128), BF16),
+            pltpu.VMEM((48, 128), F32),
             pltpu.VMEM((2, REC, 128), BF16),
             pltpu.VMEM((ZN, REC, 128), BF16),
             pltpu.VMEM((16 * REC, 128), F32),
+            pltpu.VMEM((16 * 16, 128), F32),
             pltpu.VMEM((16, 16, 128), BF16),
             pltpu.VMEM((XYN, 16, 128), BF16),
-            pltpu.VMEM((16, 128), F32),
-            pltpu.VMEM((16, 128), F32),
             pltpu.VMEM((16, 128), BF16),
             pltpu.VMEM((ZN, 16, 128), BF16),
-            pltpu.VMEM((16 * 16, 128), F32),
+            pltpu.VMEM((2 * 16, 16, 128), BF16),
             pltpu.SemaphoreType.DMA((6,)),
-            pltpu.SemaphoreType.DMA((3,)),
-            pltpu.SemaphoreType.DMA((10,)),
-            pltpu.SemaphoreType.DMA((10,)),
+            pltpu.SemaphoreType.DMA((4,)),
+            pltpu.SemaphoreType.DMA((9,)),
+            pltpu.SemaphoreType.DMA((9,)),
         ],
         compiler_params=pltpu.CompilerParams(
-            collective_id=0, has_side_effects=True, vmem_limit_bytes=48 * 1024 * 1024
+            collective_id=0, has_side_effects=True, vmem_limit_bytes=32 * 1024 * 1024
         ),
     )(*inputs)
+    token_grad, router_grad, w_in_grad, w_out_grad = pl.pallas_call(
+        store_kernel,
+        name="store",
+        out_shape=results,
+        in_specs=[anywhere] * 4,
+        out_specs=(hbm,) * 4,
+        scratch_shapes=[pltpu.SemaphoreType.DMA((7,))],
+    )(*(pltpu.with_memory_space_constraint(a, pltpu.VMEM) for a in made))
+    return (token_grad, router_grad, jnp.swapaxes(w_in_grad, 1, 2), w_out_grad)
 
 
 def solution(mesh):

time: 70.4 us -> 63.7 us (0.905)
  local copies, waits for them, and re-layouts: 7.1 us -> 0 us
    unnamed x14 -> x0, local copies, waits for them, and re-layouts: 6.13 us -> none
    pallas_call x1 -> x0, local copies, waits for them, and re-layouts: 0.97 us -> none  [local(): pl.pallas_call(kernel, name='moe_back', out_shape=(jax.ShapeDtypeStruct(t...]
    pallas_call x1 -> x2, Pallas kernels: 62.1 us -> 62.8 us  [the longest x1 61.7 us: local(): pl.pallas_call(kernel, name='moe_back', out_shape=tuple((pltpu.VMEM(a.sha...]
where the time goes in v2:
time: 63.7 us; the launch traced here: 63.5 us
  Pallas kernels  62.8 us (99%)
  between operations  0.64 us (1%)
    pallas_call x1, Pallas kernels, local(): pl.pallas_call(kernel, name='moe_back', out_shape=tuple((pltpu.VMEM(a.sha...  61.7 us

profile of v2, /device:TPU:1, one launch (start us, length us, event | category | flops | bytes accessed | tf_op | source)
XLA Modules:
  0.0 63.5 jit_solution(5579698909938762053)
XLA Ops:
  0.6 61.7 %moe_back.1 = (bf16[1,256,1280]{2,1,0:T(8,128)(2,1)S(1)}, f32[16,1280]{1,0:T(8,128)S(1)}, bf16[1,160,1280]{2,1,0:T(8,128)(2,1)S(1)}, bf16[1,160,1280]{2,1,0:T(8,128)(2,1)S(1)}) custom-call(bf16[1,256,1280]{2,1,0:T(8,128)(2,1)} %tokens_hbm.1, bf16[1,256,1280]{2,1,0:T(8,128)(2,1)} %grads_hbm.1, f32[1,16,256]{2,1,0:T(8,128)} %logits_hbm.1, ...), custom_call_target="tpu_custom_call" | custom-call | tf_op jit(solution)/shard_map/moe_back/pallas_call | solution.py:323
  62.3 1.2 %store.1 = (bf16[1,256,1280]{2,1,0:T(8,128)(2,1)}, f32[16,1280]{1,0:T(8,128)}, bf16[1,160,1280]{2,1,0:T(8,128)(2,1)}, bf16[1,160,1280]{2,1,0:T(8,128)(2,1)}) custom-call(bf16[1,256,1280]{2,1,0:T(8,128)(2,1)S(1)} %get-tuple-element.12.refs_0_, f32[16,1280]{1,0:T(8,128)S(1)} %get-tuple-element.13.refs_1_, bf16[1,160,1280]{2,1,0:T(8,128)(2,1)S(1)} %get-tuple-element.14.refs_2_, ...), custom_call_target="tpu_custom_call" | custom-call | tf_op jit(solution)/shard_map/store/pallas_call | solution.py:363

commit v3 on v2

--- a/solution.py
+++ b/solution.py
@@ -37,7 +37,7 @@
     token_grad_hbm, router_grad_hbm, w_in_grad_hbm, w_out_grad_hbm,
     tokens_v, grads_v, logits_v, router_v, w_in_v, w_out_v, token_grad_v, router_grad_ref, w_in_grad_v, w_out_grad_v,
     sa, ra, sz, rz, sb, rb, wide, sc, rc, halves, sd, rd, se, rows, sf, rf, sh, rh, ri,
-    in_sem, out_sem, send_sem, recv_sem,
+    in_sem, out_sem, send_sem, recv_sem, near_sem, far_sem,
 ):
     dp, sq = lax.axis_index("dp"), lax.axis_index("seq")
     zhi, xy = dp // 16, lax.rem(dp, 16)
@@ -51,6 +51,17 @@
     z_peers = [lax.rem(z + k, ZN) for k in Z_ORDER]
     xy_peers = [lax.rem(x + dx, 4) * 4 + lax.rem(y + dy, 4) for dx, dy in XY_ORDER]
     sibling = device(z, xy, 1 - core)
+
+    barrier = pltpu.get_barrier_semaphore()
+
+    @pl.when(core == 0)
+    def _():
+        pl.semaphore_signal(barrier, inc=1, device_id=sibling, device_id_type=MESH)
+
+    for z_to in z_peers:
+        pl.semaphore_signal(barrier, inc=1, device_id=device(z_to, xy, 0), device_id_type=MESH)
+    for xy_to in xy_peers:
+        pl.semaphore_signal(barrier, inc=1, device_id=device(z, xy_to, 0), device_id_type=MESH)
 
     loads = []
     for i, (src, dst) in enumerate(
@@ -67,14 +78,10 @@
         copy.start()
         loads.append(copy)
 
-    barrier = pltpu.get_barrier_semaphore()
-    for z_to in z_peers:
-        pl.semaphore_signal(barrier, inc=1, device_id=device(z_to, xy, core), device_id_type=MESH)
-    for xy_to in xy_peers:
-        pl.semaphore_signal(barrier, inc=1, device_id=device(z, xy_to, core), device_id_type=MESH)
-    for xy_to in xy_peers:
-        pl.semaphore_signal(barrier, inc=1, device_id=device(z, xy_to, 1 - core), device_id_type=MESH)
-    pl.semaphore_signal(barrier, inc=1, device_id=sibling, device_id_type=MESH)
+    @pl.when(core == 1)
+    def _():
+        pl.semaphore_wait(barrier, 1)
+        pl.semaphore_signal(near_sem, inc=1, device_id=sibling, device_id_type=MESH)
 
     def send(stage, src, dst, to):
         pltpu.make_async_remote_copy(
@@ -122,7 +129,9 @@
     loads[4].wait()
     loads[5].wait()
 
-    pl.semaphore_wait(barrier, 46)
+    @pl.when(core == 0)
+    def _():
+        pl.semaphore_wait(near_sem, 1)
 
     send(0, sa.at[pl.ds((1 - core) * 192, 192)], ra, sibling)
     wait(recv_sem.at[0], ra)
@@ -137,6 +146,15 @@
     both = jnp.where(row == 20, top, jnp.where(row == 22, count - low(count), both))
     sz[...] = both.astype(BF16)
     rz[pl.ds(z, 1)] = sz[pl.ds(zlo, 1)]
+
+    @pl.when(core == 0)
+    def _():
+        pl.semaphore_wait(barrier, 60)
+        pl.semaphore_signal(far_sem, inc=1, device_id=sibling, device_id_type=MESH)
+
+    @pl.when(core == 1)
+    def _():
+        pl.semaphore_wait(far_sem, 1)
 
     for z_to in z_peers:
         send(1, sz.at[lax.rem(z_to, 8)], rz.at[z], device(z_to, xy, core))
@@ -355,6 +373,8 @@
             pltpu.SemaphoreType.DMA((4,)),
             pltpu.SemaphoreType.DMA((9,)),
             pltpu.SemaphoreType.DMA((9,)),
+            pltpu.SemaphoreType.REGULAR,
+            pltpu.SemaphoreType.REGULAR,
         ],
         compiler_params=pltpu.CompilerParams(
             collective_id=0, has_side_effects=True, vmem_limit_bytes=32 * 1024 * 1024

time: 63.7 us -> 62.5 us (0.981)
  Pallas kernels: 62.8 us -> 61.7 us
    pallas_call x1, Pallas kernels: 61.7 us -> 60.5 us  [local(): pl.pallas_call(kernel, name='moe_back', out_shape=tuple((pltpu.VMEM(a.sha...]
where the time goes in v3:
time: 62.5 us; the launch traced here: 62.3 us
  Pallas kernels  61.7 us (99%)
  between operations  0.64 us (1%)
    pallas_call x1, Pallas kernels, local(): pl.pallas_call(kernel, name='moe_back', out_shape=tuple((pltpu.VMEM(a.sha...  60.5 us

profile of v3, /device:TPU:1, one launch (start us, length us, event | category | flops | bytes accessed | tf_op | source)
XLA Modules:
  0.0 62.3 jit_solution(7118686590586367093)
XLA Ops:
  0.6 60.5 %moe_back.1 = (bf16[1,256,1280]{2,1,0:T(8,128)(2,1)S(1)}, f32[16,1280]{1,0:T(8,128)S(1)}, bf16[1,160,1280]{2,1,0:T(8,128)(2,1)S(1)}, bf16[1,160,1280]{2,1,0:T(8,128)(2,1)S(1)}) custom-call(bf16[1,256,1280]{2,1,0:T(8,128)(2,1)} %tokens_hbm.1, bf16[1,256,1280]{2,1,0:T(8,128)(2,1)} %grads_hbm.1, f32[1,16,256]{2,1,0:T(8,128)} %logits_hbm.1, ...), custom_call_target="tpu_custom_call" | custom-call | tf_op jit(solution)/shard_map/moe_back/pallas_call | solution.py:341
  61.1 1.2 %store.1 = (bf16[1,256,1280]{2,1,0:T(8,128)(2,1)}, f32[16,1280]{1,0:T(8,128)}, bf16[1,160,1280]{2,1,0:T(8,128)(2,1)}, bf16[1,160,1280]{2,1,0:T(8,128)(2,1)}) custom-call(bf16[1,256,1280]{2,1,0:T(8,128)(2,1)S(1)} %get-tuple-element.12.refs_0_, f32[16,1280]{1,0:T(8,128)S(1)} %get-tuple-element.13.refs_1_, bf16[1,160,1280]{2,1,0:T(8,128)(2,1)S(1)} %get-tuple-element.14.refs_2_, ...), custom_call_target="tpu_custom_call" | custom-call | tf_op jit(solution)/shard_map/store/pallas_call | solution.py:383

commit v4 on v3

--- a/solution.py
+++ b/solution.py
@@ -54,14 +54,14 @@
 
     barrier = pltpu.get_barrier_semaphore()
 
-    @pl.when(core == 0)
+    @pl.when(core == 1)
     def _():
         pl.semaphore_signal(barrier, inc=1, device_id=sibling, device_id_type=MESH)
 
     for z_to in z_peers:
-        pl.semaphore_signal(barrier, inc=1, device_id=device(z_to, xy, 0), device_id_type=MESH)
+        pl.semaphore_signal(barrier, inc=1, device_id=device(z_to, xy, 1), device_id_type=MESH)
     for xy_to in xy_peers:
-        pl.semaphore_signal(barrier, inc=1, device_id=device(z, xy_to, 0), device_id_type=MESH)
+        pl.semaphore_signal(barrier, inc=1, device_id=device(z, xy_to, 1), device_id_type=MESH)
 
     loads = []
     for i, (src, dst) in enumerate(
@@ -78,7 +78,7 @@
         copy.start()
         loads.append(copy)
 
-    @pl.when(core == 1)
+    @pl.when(core == 0)
     def _():
         pl.semaphore_wait(barrier, 1)
         pl.semaphore_signal(near_sem, inc=1, device_id=sibling, device_id_type=MESH)
@@ -129,7 +129,7 @@
     loads[4].wait()
     loads[5].wait()
 
-    @pl.when(core == 0)
+    @pl.when(core == 1)
     def _():
         pl.semaphore_wait(near_sem, 1)
 
@@ -147,12 +147,12 @@
     sz[...] = both.astype(BF16)
     rz[pl.ds(z, 1)] = sz[pl.ds(zlo, 1)]
 
-    @pl.when(core == 0)
+    @pl.when(core == 1)
     def _():
         pl.semaphore_wait(barrier, 60)
         pl.semaphore_signal(far_sem, inc=1, device_id=sibling, device_id_type=MESH)
 
-    @pl.when(core == 1)
+    @pl.when(core == 0)
     def _():
         pl.semaphore_wait(far_sem, 1)
 

time: 62.5 us -> 62.1 us (level)
  no operation moved by 1% of the time
where the time goes in v4:
time: 62.1 us; the launch traced here: 62 us
  Pallas kernels  61.3 us (99%)
  between operations  0.64 us (1%)
    pallas_call x1, Pallas kernels, local(): pl.pallas_call(kernel, name='moe_back', out_shape=tuple((pltpu.VMEM(a.sha...  60.1 us

profile of v4, /device:TPU:1, one launch (start us, length us, event | category | flops | bytes accessed | tf_op | source)
XLA Modules:
  0.0 62.0 jit_solution(4644340896234148245)
XLA Ops:
  0.6 60.1 %moe_back.1 = (bf16[1,256,1280]{2,1,0:T(8,128)(2,1)S(1)}, f32[16,1280]{1,0:T(8,128)S(1)}, bf16[1,160,1280]{2,1,0:T(8,128)(2,1)S(1)}, bf16[1,160,1280]{2,1,0:T(8,128)(2,1)S(1)}) custom-call(bf16[1,256,1280]{2,1,0:T(8,128)(2,1)} %tokens_hbm.1, bf16[1,256,1280]{2,1,0:T(8,128)(2,1)} %grads_hbm.1, f32[1,16,256]{2,1,0:T(8,128)} %logits_hbm.1, ...), custom_call_target="tpu_custom_call" | custom-call | tf_op jit(solution)/shard_map/moe_back/pallas_call | solution.py:341
  60.8 1.2 %store.1 = (bf16[1,256,1280]{2,1,0:T(8,128)(2,1)}, f32[16,1280]{1,0:T(8,128)}, bf16[1,160,1280]{2,1,0:T(8,128)(2,1)}, bf16[1,160,1280]{2,1,0:T(8,128)(2,1)}) custom-call(bf16[1,256,1280]{2,1,0:T(8,128)(2,1)S(1)} %get-tuple-element.12.refs_0_, f32[16,1280]{1,0:T(8,128)S(1)} %get-tuple-element.13.refs_1_, bf16[1,160,1280]{2,1,0:T(8,128)(2,1)S(1)} %get-tuple-element.14.refs_2_, ...), custom_call_target="tpu_custom_call" | custom-call | tf_op jit(solution)/shard_map/store/pallas_call | solution.py:383

commit v5 on v4

--- a/solution.py
+++ b/solution.py
@@ -34,9 +34,9 @@
 
 def kernel(
     tokens_hbm, grads_hbm, logits_hbm, router_hbm, w_in_hbm, w_out_hbm,
-    token_grad_hbm, router_grad_hbm, w_in_grad_hbm, w_out_grad_hbm,
-    tokens_v, grads_v, logits_v, router_v, w_in_v, w_out_v, token_grad_v, router_grad_ref, w_in_grad_v, w_out_grad_v,
-    sa, ra, sz, rz, sb, rb, wide, sc, rc, halves, sd, rd, se, rows, sf, rf, sh, rh, ri,
+    token_grad_hbm, ri, w_in_grad_hbm, w_out_grad_hbm,
+    tokens_v, grads_v, logits_v, router_v, w_in_v, w_out_v, token_grad_v, w_in_grad_v, w_out_grad_v,
+    sa, ra, sz, rz, sb, rb, wide, sc, rc, halves, sd, rd, se, rows, sf, rf, own_row, other_row, sh, rh, summed_row,
     in_sem, out_sem, send_sem, recv_sem, near_sem, far_sem,
 ):
     dp, sq = lax.axis_index("dp"), lax.axis_index("seq")
@@ -218,7 +218,6 @@
         pltpu.make_async_copy(w_in_grad_v, w_in_grad_hbm, out_sem.at[0]),
         pltpu.make_async_copy(w_out_grad_v, w_out_grad_hbm, out_sem.at[1]),
         pltpu.make_async_copy(token_grad_v, token_grad_hbm, out_sem.at[2]),
-        pltpu.make_async_copy(router_grad_ref, router_grad_hbm, out_sem.at[3]),
     ]
     stores[0].start()
     stores[1].start()
@@ -277,24 +276,24 @@
     token_grad_v[0] = (dot(left, right, ((0,), (0,))) * 64.0).astype(BF16)
     stores[2].start()
     wait(recv_sem.at[6], rf.at[pl.ds(0, XYN - 1)])
-    sh[...] = jnp.sum(rf[...].astype(F32), axis=0).astype(BF16)
+    own_row[...] = jnp.sum(rf[...].astype(F32), axis=0)
+    send(9, own_row, other_row, sibling)
+    wait(recv_sem.at[9], other_row)
+    sh[...] = (own_row[...] + other_row[...]).astype(BF16)
     rh[pl.ds(z, 1)] = sh[...][None]
 
     for z_to in z_peers:
         send(7, sh, rh.at[z], device(z_to, xy, core))
     wait(recv_sem.at[7], rh.at[pl.ds(0, ZN - 1)])
-    place = core * 16 + lax.rem(xy, 8) * 2 + xy // 8
-    ri[pl.ds(place, 1)] = jnp.sum(rh[...].astype(F32), axis=0).astype(BF16)[None]
+    place = lax.rem(xy, 8) * 2 + xy // 8
+    summed_row[...] = jnp.sum(rh[...].astype(F32), axis=0, keepdims=True).astype(BF16)
 
     for xy_to in xy_peers:
-        send(8, ri.at[place], ri.at[place], device(z, xy_to, core))
-        send(8, ri.at[place], ri.at[place], device(z, xy_to, 1 - core))
-    send(8, ri.at[place], ri.at[place], sibling)
-    wait(recv_sem.at[8], ri.at[pl.ds(0, 31)])
-    rows[...] = ((ri[pl.ds(0, 16)].astype(F32) + ri[pl.ds(16, 16)].astype(F32)) / math.sqrt(32.0)).reshape(256, 128)
-    for j in range(CH):
-        router_grad_ref[:, j * 128 : (j + 1) * 128] = rows[pl.ds(j, 16, stride=16), :]
-    stores[3].start()
+        send(8, summed_row.at[0], ri.at[place], device(z, xy_to, core))
+    kept = pltpu.make_async_copy(summed_row.at[0], ri.at[place], out_sem.at[3])
+    kept.start()
+    stores.append(kept)
+    wait(recv_sem.at[8], ri.at[pl.ds(0, 15)])
 
     wait(send_sem.at[0], ra)
     wait(send_sem.at[1], rz.at[pl.ds(0, ZN - 1)])
@@ -304,23 +303,32 @@
     wait(send_sem.at[5], ra)
     wait(send_sem.at[6], rf.at[pl.ds(0, XYN - 1)])
     wait(send_sem.at[7], rh.at[pl.ds(0, ZN - 1)])
-    wait(send_sem.at[8], ri.at[pl.ds(0, 31)])
+    wait(send_sem.at[8], ri.at[pl.ds(0, 15)])
+    wait(send_sem.at[9], other_row)
     for copy in stores:
         copy.wait()
 
 
-def store_kernel(*refs):
-    sources, targets, sems = refs[:4], refs[4:8], refs[8]
-    copies = []
-    for a, b in zip(sources, targets):
-        if len(a.shape) == 2:
-            parts = [(a, b)]
-        else:
-            cut = a.shape[1] // 2
-            parts = [(a.at[:, pl.ds(i * cut, cut)], b.at[:, pl.ds(i * cut, cut)]) for i in range(2)]
-        for part, to in parts:
-            copies.append(pltpu.make_async_copy(part, to, sems.at[len(copies)]))
-            copies[-1].start()
+def store_kernel(
+    token_grad, ri, w_in_grad, w_out_grad,
+    token_grad_hbm, router_grad_hbm, w_in_grad_hbm, w_out_grad_hbm,
+    ri_v, rows, router_grad_v, sems,
+):
+    gather = pltpu.make_async_copy(ri, ri_v, sems.at[0])
+    gather.start()
+    copies = [
+        pltpu.make_async_copy(token_grad, token_grad_hbm, sems.at[1]),
+        pltpu.make_async_copy(w_in_grad, w_in_grad_hbm, sems.at[2]),
+        pltpu.make_async_copy(w_out_grad, w_out_grad_hbm, sems.at[3]),
+        pltpu.make_async_copy(router_grad_v, router_grad_hbm, sems.at[4]),
+    ]
+    for copy in copies[:3]:
+        copy.start()
+    gather.wait()
+    rows[...] = (ri_v[...].astype(F32) / math.sqrt(32.0)).reshape(256, 128)
+    for j in range(CH):
+        router_grad_v[:, j * 128 : (j + 1) * 128] = rows[pl.ds(j, 16, stride=16), :]
+    copies[3].start()
     for copy in copies:
         copy.wait()
 
@@ -341,13 +349,14 @@
     made = pl.pallas_call(
         kernel,
         name="moe_back",
-        out_shape=tuple(pltpu.VMEM(a.shape, a.dtype) for a in results),
+        out_shape=tuple(
+            pltpu.VMEM(shape, BF16) for shape in (tokens.shape, (16, 16, 128), w_in.shape, w_out.shape)
+        ),
         in_specs=[hbm] * 6,
         out_specs=(anywhere,) * 4,
         scratch_shapes=[pltpu.VMEM(a.shape, a.dtype) for a in inputs]
         + [
             pltpu.VMEM(tokens.shape, BF16),
-            pltpu.VMEM(router.shape, F32),
             pltpu.VMEM(w_in.shape, BF16),
             pltpu.VMEM(w_out.shape, BF16),
             pltpu.VMEM((16 * REC, 128), F32),
@@ -366,13 +375,15 @@
             pltpu.VMEM((16 * 16, 128), F32),
             pltpu.VMEM((16, 16, 128), BF16),
             pltpu.VMEM((XYN, 16, 128), BF16),
+            pltpu.VMEM((16, 128), F32),
+            pltpu.VMEM((16, 128), F32),
             pltpu.VMEM((16, 128), BF16),
             pltpu.VMEM((ZN, 16, 128), BF16),
-            pltpu.VMEM((2 * 16, 16, 128), BF16),
+            pltpu.VMEM((1, 16, 128), BF16),
             pltpu.SemaphoreType.DMA((6,)),
             pltpu.SemaphoreType.DMA((4,)),
-            pltpu.SemaphoreType.DMA((9,)),
-            pltpu.SemaphoreType.DMA((9,)),
+            pltpu.SemaphoreType.DMA((10,)),
+            pltpu.SemaphoreType.DMA((10,)),
             pltpu.SemaphoreType.REGULAR,
             pltpu.SemaphoreType.REGULAR,
         ],
@@ -386,7 +397,12 @@
         out_shape=results,
         in_specs=[anywhere] * 4,
         out_specs=(hbm,) * 4,
-        scratch_shapes=[pltpu.SemaphoreType.DMA((7,))],
+        scratch_shapes=[
+            pltpu.VMEM((16, 16, 128), BF16),
+            pltpu.VMEM((256, 128), F32),
+            pltpu.VMEM(router.shape, F32),
+            pltpu.SemaphoreType.DMA((5,)),
+        ],
     )(*(pltpu.with_memory_space_constraint(a, pltpu.VMEM) for a in made))
     return (token_grad, router_grad, jnp.swapaxes(w_in_grad, 1, 2), w_out_grad)
 

time: 62.1 us -> 61.5 us (level)
  Pallas kernels: 61.3 us -> 60.5 us
    pallas_call x1, Pallas kernels: 60.1 us -> 59.3 us  [local(): pl.pallas_call(kernel, name='moe_back', out_shape=tuple((pltpu.VMEM(shape...]
where the time goes in v5:
time: 61.5 us; the launch traced here: 61.2 us
  Pallas kernels  60.5 us (98%)
  between operations  0.64 us (1%)
    pallas_call x1, Pallas kernels, local(): pl.pallas_call(kernel, name='moe_back', out_shape=tuple((pltpu.VMEM(shape...  59.3 us
    pallas_call x1, Pallas kernels, local(): pl.pallas_call(store_kernel, name='store', out_shape=results, in_specs=[a...  1.25 us

profile of v5, /device:TPU:1, one launch (start us, length us, event | category | flops | bytes accessed | tf_op | source)
XLA Modules:
  0.0 61.2 jit_solution(6831705715782659480)
XLA Ops:
  0.6 59.3 %moe_back.1 = (bf16[1,256,1280]{2,1,0:T(8,128)(2,1)S(1)}, bf16[16,16,128]{2,1,0:T(8,128)(2,1)S(1)}, bf16[1,160,1280]{2,1,0:T(8,128)(2,1)S(1)}, bf16[1,160,1280]{2,1,0:T(8,128)(2,1)S(1)}) custom-call(bf16[1,256,1280]{2,1,0:T(8,128)(2,1)} %tokens_hbm.1, bf16[1,256,1280]{2,1,0:T(8,128)(2,1)} %grads_hbm.1, f32[1,16,256]{2,1,0:T(8,128)} %logits_hbm.1, ...), custom_call_target="tpu_custom_call" | custom-call | tf_op jit(solution)/shard_map/moe_back/pallas_call | solution.py:349
  59.9 1.2 %store.1 = (bf16[1,256,1280]{2,1,0:T(8,128)(2,1)}, f32[16,1280]{1,0:T(8,128)}, bf16[1,160,1280]{2,1,0:T(8,128)(2,1)}, bf16[1,160,1280]{2,1,0:T(8,128)(2,1)}) custom-call(bf16[1,256,1280]{2,1,0:T(8,128)(2,1)S(1)} %get-tuple-element.12.token_grad, bf16[16,16,128]{2,1,0:T(8,128)(2,1)S(1)} %get-tuple-element.13.ri, ...), custom_call_target="tpu_custom_call" | custom-call | tf_op jit(solution)/shard_map/store/pallas_call | solution.py:394

commit v6 on v5

--- a/solution.py
+++ b/solution.py
@@ -18,7 +18,7 @@
 REC = 24
 ZN = 16
 XYN = 16
-Z_ORDER = (8, 7, 9, 6, 10, 5, 11, 4, 12, 3, 13, 2, 14, 1, 15)
+Z_ORDER = (8, 9, 7, 10, 6, 11, 5, 12, 4, 13, 3, 14, 2, 15, 1)
 XY_ORDER = (
     (2, 2), (2, 1), (2, 3), (1, 2), (3, 2), (1, 1), (1, 3), (3, 1), (3, 3), (2, 0), (0, 2), (1, 0), (3, 0), (0, 1), (0, 3),
 )
@@ -77,11 +77,6 @@
         copy = pltpu.make_async_copy(src, dst, in_sem.at[i])
         copy.start()
         loads.append(copy)
-
-    @pl.when(core == 0)
-    def _():
-        pl.semaphore_wait(barrier, 1)
-        pl.semaphore_signal(near_sem, inc=1, device_id=sibling, device_id_type=MESH)
 
     def send(stage, src, dst, to):
         pltpu.make_async_remote_copy(
@@ -128,6 +123,11 @@
     router = core_major(router_v[...].astype(F32))
     loads[4].wait()
     loads[5].wait()
+
+    @pl.when(core == 0)
+    def _():
+        pl.semaphore_wait(barrier, 1)
+        pl.semaphore_signal(near_sem, inc=1, device_id=sibling, device_id_type=MESH)
 
     @pl.when(core == 1)
     def _():

time: 61.5 us -> 61.1 us (level)
  no operation moved by 1% of the time
where the time goes in v6:
time: 61.1 us; the launch traced here: 60.9 us
  Pallas kernels  60.2 us (99%)
  between operations  0.64 us (1%)
    pallas_call x1, Pallas kernels, local(): pl.pallas_call(kernel, name='moe_back', out_shape=tuple((pltpu.VMEM(shape...  59 us
    pallas_call x1, Pallas kernels, local(): pl.pallas_call(store_kernel, name='store', out_shape=results, in_specs=[a...  1.25 us

profile of v6, /device:TPU:1, one launch (start us, length us, event | category | flops | bytes accessed | tf_op | source)
XLA Modules:
  0.0 60.9 jit_solution(12700168183189140845)
XLA Ops:
  0.6 59.0 %moe_back.1 = (bf16[1,256,1280]{2,1,0:T(8,128)(2,1)S(1)}, bf16[16,16,128]{2,1,0:T(8,128)(2,1)S(1)}, bf16[1,160,1280]{2,1,0:T(8,128)(2,1)S(1)}, bf16[1,160,1280]{2,1,0:T(8,128)(2,1)S(1)}) custom-call(bf16[1,256,1280]{2,1,0:T(8,128)(2,1)} %tokens_hbm.1, bf16[1,256,1280]{2,1,0:T(8,128)(2,1)} %grads_hbm.1, f32[1,16,256]{2,1,0:T(8,128)} %logits_hbm.1, ...), custom_call_target="tpu_custom_call" | custom-call | tf_op jit(solution)/shard_map/moe_back/pallas_call | solution.py:349
  59.6 1.2 %store.1 = (bf16[1,256,1280]{2,1,0:T(8,128)(2,1)}, f32[16,1280]{1,0:T(8,128)}, bf16[1,160,1280]{2,1,0:T(8,128)(2,1)}, bf16[1,160,1280]{2,1,0:T(8,128)(2,1)}) custom-call(bf16[1,256,1280]{2,1,0:T(8,128)(2,1)S(1)} %get-tuple-element.12.token_grad, bf16[16,16,128]{2,1,0:T(8,128)(2,1)S(1)} %get-tuple-element.13.ri, ...), custom_call_target="tpu_custom_call" | custom-call | tf_op jit(solution)/shard_map/store/pallas_call | solution.py:394

commit v7 on v6

--- a/solution.py
+++ b/solution.py
@@ -34,8 +34,8 @@
 
 def kernel(
     tokens_hbm, grads_hbm, logits_hbm, router_hbm, w_in_hbm, w_out_hbm,
-    token_grad_hbm, ri, w_in_grad_hbm, w_out_grad_hbm,
-    tokens_v, grads_v, logits_v, router_v, w_in_v, w_out_v, token_grad_v, w_in_grad_v, w_out_grad_v,
+    token_grad_v, ri, w_in_grad_v, w_out_grad_v,
+    tokens_v, grads_v, logits_v, router_v, w_in_v, w_out_v,
     sa, ra, sz, rz, sb, rb, wide, sc, rc, halves, sd, rd, se, rows, sf, rf, own_row, other_row, sh, rh, summed_row,
     in_sem, out_sem, send_sem, recv_sem, near_sem, far_sem,
 ):
@@ -214,13 +214,6 @@
         send(3, sc.at[xy_to], rc.at[xy], device(z, xy_to, core))
     w_out_grad_v[0] = dot(activated, every_back, ((0,), (0,))).astype(BF16)
     w_in_grad_v[0] = dot(hidden_back, every_in, ((0,), (0,))).astype(BF16)
-    stores = [
-        pltpu.make_async_copy(w_in_grad_v, w_in_grad_hbm, out_sem.at[0]),
-        pltpu.make_async_copy(w_out_grad_v, w_out_grad_hbm, out_sem.at[1]),
-        pltpu.make_async_copy(token_grad_v, token_grad_hbm, out_sem.at[2]),
-    ]
-    stores[0].start()
-    stores[1].start()
     wait(recv_sem.at[3], rc.at[pl.ds(0, XYN - 1)])
     halves[pl.ds(0, PAIR), :] = jnp.sum(rc[...].astype(F32), axis=0)
     for h in range(2):
@@ -274,7 +267,6 @@
     left = jnp.concatenate([weights, logit_back.astype(F32)], axis=0).astype(BF16)
     right = jnp.concatenate([in_back.astype(F32), router], axis=0).astype(BF16)
     token_grad_v[0] = (dot(left, right, ((0,), (0,))) * 64.0).astype(BF16)
-    stores[2].start()
     wait(recv_sem.at[6], rf.at[pl.ds(0, XYN - 1)])
     own_row[...] = jnp.sum(rf[...].astype(F32), axis=0)
     send(9, own_row, other_row, sibling)
@@ -290,9 +282,8 @@
 
     for xy_to in xy_peers:
         send(8, summed_row.at[0], ri.at[place], device(z, xy_to, core))
-    kept = pltpu.make_async_copy(summed_row.at[0], ri.at[place], out_sem.at[3])
+    kept = pltpu.make_async_copy(summed_row.at[0], ri.at[place], out_sem.at[0])
     kept.start()
-    stores.append(kept)
     wait(recv_sem.at[8], ri.at[pl.ds(0, 15)])
 
     wait(send_sem.at[0], ra)
@@ -305,8 +296,7 @@
     wait(send_sem.at[7], rh.at[pl.ds(0, ZN - 1)])
     wait(send_sem.at[8], ri.at[pl.ds(0, 15)])
     wait(send_sem.at[9], other_row)
-    for copy in stores:
-        copy.wait()
+    kept.wait()
 
 
 def store_kernel(
@@ -335,6 +325,7 @@
 
 def local(tokens, out_grad, logits, router, w_in, w_out):
     anywhere = pl.BlockSpec(memory_space=pl.ANY)
+    vmem = pl.BlockSpec(memory_space=pltpu.VMEM)
     hbm = pl.BlockSpec(memory_space=pltpu.HBM)
     w_in = jnp.swapaxes(w_in, 1, 2)
     inputs = tuple(
@@ -353,12 +344,9 @@
             pltpu.VMEM(shape, BF16) for shape in (tokens.shape, (16, 16, 128), w_in.shape, w_out.shape)
         ),
         in_specs=[hbm] * 6,
-        out_specs=(anywhere,) * 4,
+        out_specs=(vmem, anywhere, vmem, vmem),
         scratch_shapes=[pltpu.VMEM(a.shape, a.dtype) for a in inputs]
         + [
-            pltpu.VMEM(tokens.shape, BF16),
-            pltpu.VMEM(w_in.shape, BF16),
-            pltpu.VMEM(w_out.shape, BF16),
             pltpu.VMEM((16 * REC, 128), F32),
             pltpu.VMEM((8 * REC, 128), F32),
             pltpu.VMEM((8, REC, 128), BF16),

time: 61.1 us -> 61 us (level)
  no operation moved by 1% of the time
where the time goes in v7:
time: 61 us; the launch traced here: 60.9 us
  Pallas kernels  60.2 us (99%)
  between operations  0.64 us (1%)
    pallas_call x1, Pallas kernels, local(): pl.pallas_call(kernel, name='moe_back', out_shape=tuple((pltpu.VMEM(shape...  59 us
    pallas_call x1, Pallas kernels, local(): pl.pallas_call(store_kernel, name='store', out_shape=results, in_specs=[a...  1.25 us

profile of v7, /device:TPU:1, one launch (start us, length us, event | category | flops | bytes accessed | tf_op | source)
XLA Modules:
  0.0 60.9 jit_solution(2653009081333406460)
XLA Ops:
  0.6 59.0 %moe_back.1 = (bf16[1,256,1280]{2,1,0:T(8,128)(2,1)S(1)}, bf16[16,16,128]{2,1,0:T(8,128)(2,1)S(1)}, bf16[1,160,1280]{2,1,0:T(8,128)(2,1)S(1)}, bf16[1,160,1280]{2,1,0:T(8,128)(2,1)S(1)}) custom-call(bf16[1,256,1280]{2,1,0:T(8,128)(2,1)} %tokens_hbm.1, bf16[1,256,1280]{2,1,0:T(8,128)(2,1)} %grads_hbm.1, f32[1,16,256]{2,1,0:T(8,128)} %logits_hbm.1, ...), custom_call_target="tpu_custom_call" | custom-call | tf_op jit(solution)/shard_map/moe_back/pallas_call | solution.py:340
  59.6 1.2 %store.1 = (bf16[1,256,1280]{2,1,0:T(8,128)(2,1)}, f32[16,1280]{1,0:T(8,128)}, bf16[1,160,1280]{2,1,0:T(8,128)(2,1)}, bf16[1,160,1280]{2,1,0:T(8,128)(2,1)}) custom-call(bf16[1,256,1280]{2,1,0:T(8,128)(2,1)S(1)} %get-tuple-element.12.token_grad, bf16[16,16,128]{2,1,0:T(8,128)(2,1)S(1)} %get-tuple-element.13.ri, ...), custom_call_target="tpu_custom_call" | custom-call | tf_op jit(solution)/shard_map/store/pallas_call | solution.py:382
